TPU v7x, 256 devices: a whole 4x4x8 slice. The times are simulated.
256 devices in a mesh: grp: 8 (over y, z_hi), ep: 32 (over x, z_lo, core).
Axes of the slice: x: 4, y: 4, z: 8 (z_hi: 2, z_lo: 4; z = z_hi * 4 + z_lo), core: 2. Of those that a mesh axis runs over, the one named last changes fastest.
Arguments:
- tokens: bfloat16 [4096, 5120], P('ep', 'grp'), may hold values from -6 to 6
- out_grad: bfloat16 [4096, 5120], P('ep', 'grp'), may hold values from -1.5 to 1.5
- expert_ids: int32 [4096, 6], P('ep'), may hold values from 0 to 23, all different within a row; in each aligned block of 128 rows (0 to 127, 128 to 255, ...) at most 40 rows name the same one
- route_probs: bfloat16 [4096, 6], P('ep'), may hold values from 0.049804688 to 0.59765625
- slot_expert: int32 [32], replicated, may hold values from 0 to 23, as said below
- w_gate: bfloat16 [32, 5120, 1024], P('ep', 'grp'), as said below
- w_up: bfloat16 [32, 5120, 1024], P('ep', 'grp'), as said below
- w_down: bfloat16 [32, 5120, 1024], P('ep', 'grp'), as said below
Outputs:
- in_grad: bfloat16 [4096, 5120], P('ep', 'grp')
- grad_gate: bfloat16 [32, 5120, 1024], P('ep', 'grp')
- grad_up: bfloat16 [32, 5120, 1024], P('ep', 'grp')
- grad_down: bfloat16 [32, 5120, 1024], P('ep', 'grp')
Inputs may be any that keep to these rules, and one draw needn't show every extreme that they name: `expert_ids`: in the rows of one index of ep, no expert is named by more than 40 tokens; some expert is named by exactly 40 in some block. `slot_expert`: every expert 0 to 23 is held by at least one of the 32 slots. `w_gate`: slots that hold the same expert hold equal weights. `w_up`: slots that hold the same expert hold equal weights. `w_down`: slots that hold the same expert hold equal weights.
All inputs are finite; a program needn't handle non-finite values.
Results may differ from a plain program's by a relative error of at most 0.03.
Values may be sent and summed in bfloat16 or wider, within the bound.
No kernel may reach another device: no remote copies, remote signals or barrier semaphores. Data moves between devices by JAX's collectives and lax.ppermute only.
A program may use at most 128 MiB of HBM per device.

v0:
```python
import jax
import jax.numpy as jnp
from jax import lax
from jax.sharding import PartitionSpec as P


def activate(gate, up_sum, grad_hidden):
    sigma = jax.nn.sigmoid(gate)
    swish = gate * sigma
    hidden = (swish * up_sum).astype(jnp.bfloat16)
    grad_up = (grad_hidden * swish).astype(jnp.bfloat16)
    grad_gate = (grad_hidden * up_sum * sigma * (1.0 + gate * (1.0 - sigma))).astype(jnp.bfloat16)
    return (hidden, grad_gate, grad_up)


def per_device(tokens, out_grad, expert_ids, route_probs, slot_expert, w_gate, w_up, w_down):
    tok_count, width_part = tokens.shape
    top_count = expert_ids.shape[1]
    num_slots = lax.axis_size("ep")
    in_flight = 3 * num_slots // 4
    capacity = (30 * tok_count + 4 * in_flight - 1) // (4 * in_flight)
    slot_rows = num_slots * capacity
    slot_ids = jnp.arange(num_slots, dtype=jnp.int32)
    same_expert = (slot_expert[:, None] == slot_expert[None, :]).astype(jnp.int32)
    earlier = (slot_ids[:, None] > slot_ids[None, :]).astype(jnp.int32)
    replica_rank = jnp.sum(same_expert * earlier, axis=1)
    flat_ids = expert_ids.reshape(-1)
    hosting = flat_ids[:, None] == slot_expert[None, :]
    replicas = jnp.sum(hosting.astype(jnp.int32), axis=1)
    replica = lax.axis_index("ep") % replicas
    chosen = (hosting & (replica_rank[None, :] == replica[:, None])).astype(jnp.int32)
    target = jnp.sum(chosen * slot_ids[None, :], axis=1)
    position = jnp.sum((jnp.cumsum(chosen, axis=0) - 1) * chosen, axis=1)
    buffer_index = target * capacity + position
    send_tokens = (
        jnp.zeros((slot_rows, width_part), jnp.bfloat16)
        .at[buffer_index]
        .set(jnp.repeat(tokens, top_count, axis=0))
    )
    send_grads = (
        jnp.zeros((slot_rows, width_part), jnp.bfloat16)
        .at[buffer_index]
        .set(jnp.repeat(out_grad, top_count, axis=0))
    )
    send_probs = jnp.zeros((slot_rows,), jnp.bfloat16).at[buffer_index].set(route_probs.reshape(-1))
    recv_tokens, recv_grads, recv_probs = (
        lax.all_to_all(
            send_tokens.reshape(num_slots, capacity, width_part),
            "ep",
            split_axis=0,
            concat_axis=0,
            tiled=True,
        ),
        lax.all_to_all(
            send_grads.reshape(num_slots, capacity, width_part),
            "ep",
            split_axis=0,
            concat_axis=0,
            tiled=True,
        ),
        lax.all_to_all(
            send_probs.reshape(num_slots, capacity), "ep", split_axis=0, concat_axis=0, tiled=True
        ),
    )
    inputs = recv_tokens.reshape(slot_rows, width_part)
    scaled = (
        recv_probs.reshape(slot_rows, 1).astype(jnp.float32)
        * recv_grads.reshape(slot_rows, width_part)
    ).astype(jnp.bfloat16)
    gate_rows = w_gate[0]
    up_rows = w_up[0]
    down_rows = w_down[0]
    gate_part = jnp.dot(inputs, gate_rows, preferred_element_type=jnp.float32)
    up_part = jnp.dot(inputs, up_rows, preferred_element_type=jnp.float32)
    hidden_part = jnp.dot(scaled, down_rows, preferred_element_type=jnp.float32)
    gate, up_sum, grad_hidden = (
        lax.psum(gate_part.astype(jnp.bfloat16), "grp").astype(jnp.float32),
        lax.psum(up_part.astype(jnp.bfloat16), "grp").astype(jnp.float32),
        lax.psum(hidden_part.astype(jnp.bfloat16), "grp").astype(jnp.float32),
    )
    hidden, grad_gate, grad_up = activate(gate, up_sum, grad_hidden)
    part_gate = jnp.dot(inputs.T, grad_gate, preferred_element_type=jnp.float32).astype(
        jnp.bfloat16
    )
    part_up = jnp.dot(inputs.T, grad_up, preferred_element_type=jnp.float32).astype(jnp.bfloat16)
    part_down = jnp.dot(scaled.T, hidden, preferred_element_type=jnp.float32).astype(jnp.bfloat16)
    row_grad = (
        jnp.dot(grad_gate, gate_rows.T, preferred_element_type=jnp.float32)
        + jnp.dot(grad_up, up_rows.T, preferred_element_type=jnp.float32)
    ).astype(jnp.bfloat16)
    returned = lax.all_to_all(
        row_grad.reshape(num_slots, capacity, width_part),
        "ep",
        split_axis=0,
        concat_axis=0,
        tiled=True,
    )
    gathered = returned.reshape(slot_rows, width_part)[buffer_index]
    in_grad = jnp.sum(
        gathered.astype(jnp.float32).reshape(tok_count, top_count, width_part), axis=1
    ).astype(jnp.bfloat16)
    stacked = jnp.stack([part_gate, part_up, part_down])[None]
    mixing = same_expert.astype(jnp.bfloat16)
    mixed = jnp.einsum(
        "st,tkrh->skrh",
        mixing,
        lax.all_to_all(stacked, "ep", split_axis=2, concat_axis=0, tiled=True),
        preferred_element_type=jnp.float32,
    ).astype(jnp.bfloat16)
    summed = lax.all_to_all(mixed, "ep", split_axis=0, concat_axis=2, tiled=True)
    return (in_grad, summed[:, 0], summed[:, 1], summed[:, 2])


def solution(mesh):
    return jax.shard_map(
        per_device,
        mesh=mesh,
        in_specs=(
            P("ep", "grp"),
            P("ep", "grp"),
            P("ep", None),
            P("ep", None),
            P(),
            P("ep", "grp", None),
            P("ep", "grp", None),
            P("ep", "grp", None),
        ),
        out_specs=(
            P("ep", "grp"),
            P("ep", "grp", None),
            P("ep", "grp", None),
            P("ep", "grp", None),
        ),
        check_vma=False,
    )
```

profile of v0, /device:TPU:1, one launch (start us, length us, event | category | flops | bytes accessed | tf_op | source)
XLA Modules:
  0.0 1098.1 jit_solution(3408724642398284460)
XLA Ops:
  14.8 8.6 scatter_custom_fusion
  24.2 10.0 all-to-all-start
  36.4 7.5 scatter_custom_fusion.2
  43.9 8.2 all-to-all-start.2
  53.4 7.4 scatter_custom_fusion.1
  60.8 31.3 %all-to-all-done.2 = bf16[32,40,640]{2,1,0:T(8,128)(2,1)} async-done(((bf16[32,40,640]{2,1,0:T(8,128)(2,1)}), bf16[32,40,640]{2,1,0:T(8,128)(2,1)}, u32[]{:S(2)}, u32[]{:S(2)}) %all-to-all-start.2) | async-done | bytes 1638432 | tf_op jit(solution)/shard_map/all_to_all | solution.py:47
  92.2 4.2 all-to-all-start.1
  96.5 5.3 convolution_convert_fusion
  101.8 5.2 convolution_convert_fusion.1
  107.0 29.8 %all-to-all-done.1 = bf16[32,40,640]{2,1,0:T(8,128)(2,1)S(1)} async-done(((bf16[32,40,640]{2,1,0:T(8,128)(2,1)}), bf16[32,40,640]{2,1,0:T(8,128)(2,1)S(1)}, u32[]{:S(2)}, u32[]{:S(2)}) %all-to-all-start.1) | async-done | bytes 1638432 | tf_op jit(solution)/shard_map/all_to_all | solution.py:54
  143.5 629.0 %all-reduce.3.cloned.1.call-done = (bf16[1280,1024]{1,0:T(8,128)(2,1)}, bf16[1280,1024]{1,0:T(8,128)(2,1)}, bf16[1280,1024]{1,0:T(8,128)(2,1)}) async-done(((bf16[1280,1024]{1,0:T(8,128)(2,1)}, bf16[1280,1024]{1,0:T(8,128)(2,1)}, bf16[1280,1024]{1,0:T(8,128)(2,1)}), (bf16[1280,1024]{1,0:T(8,128)(2,1)}, bf16[1280,1024]{1,0:T(8,128)(2,1)}, bf16[1280,1024]{1,0:T(8,128)(2,1)})) %all-reduce.3.cloned.1.call-update) | async-done | bytes 7864336 | tf_op jit(solution)/shard_map/psum | solution.py:78
  772.5 5.3 fusion.24
  781.3 4.6 fusion.23
  789.7 5.7 copy.24
  795.5 6.3 all-to-all-start.4
  809.5 109.1 %all-to-all-done.4 = bf16[1,3,640,1024]{3,1,0,2:T(4,128)(2,1)} async-done(((bf16[1,3,640,1024]{3,1,0,2:T(4,128)(2,1)}), bf16[1,3,640,1024]{3,1,0,2:T(4,128)(2,1)}, u32[]{:S(2)}, u32[]{:S(2)}) %all-to-all-start.4) | async-done | bytes 3932192 | tf_op jit(solution)/shard_map/all_to_all | solution.py:107
  918.6 4.8 all-to-all-start.3
  923.4 7.9 fusion.16
  931.3 4.4 copy.27
  935.7 28.0 %all-to-all-done.3 = bf16[32,40,640]{2,1,0:T(8,128)(2,1)S(1)} async-done(((bf16[32,40,640]{2,1,0:T(8,128)(2,1)}), bf16[32,40,640]{2,1,0:T(8,128)(2,1)S(1)}, u32[]{:S(2)}, u32[]{:S(2)}) %all-to-all-start.3) | async-done | bytes 1638432 | tf_op jit(solution)/shard_map/all_to_all | solution.py:91
  963.8 5.4 all-to-all-start.5
  976.2 98.6 %all-to-all-done.5 = bf16[32,3,20,1024]{3,2,1,0:T(8,128)(2,1)} async-done(((bf16[32,3,20,1024]{3,2,1,0:T(8,128)(2,1)}), bf16[32,3,20,1024]{3,2,1,0:T(8,128)(2,1)}, u32[]{:S(2)}, u32[]{:S(2)}) %all-to-all-start.5) | async-done | bytes 3932192 | tf_op jit(solution)/shard_map/all_to_all | solution.py:110
  1074.8 5.2 copy.28
  1080.0 6.9 all_to_all.53
  (64 shorter events, 44.7 us)
Async XLA Ops:
  7.2 89.3 %copy-start = (bf16[1,640,1024]{2,1,0:T(8,128)(2,1)S(1)}, bf16[1,640,1024]{2,1,0:T(8,128)(2,1)}, u32[]{:S(2)}) copy-start(bf16[1,640,1024]{2,1,0:T(8,128)(2,1)} %param.13) | copy-start | bytes 3932164
  24.2 19.7 %all-to-all-start = ((bf16[32,1,40]{2,1,0:T(2,128)(2,1)}), bf16[32,1,40]{2,1,0:T(2,128)(2,1)S(1)}, u32[]{:S(2)}, u32[]{:S(2)}) async-start(bf16[32,1,40]{2,1,0:T(2,128)(2,1)} %all_to_all.54), calls=%async_computation | async-start | bytes 32768 | tf_op jit(solution)/shard_map/all_to_all | solution.py:61
  36.4 15.6 %copy-start.7 = (bf16[128,640]{1,0:T(8,128)(2,1)S(1)}, bf16[128,640]{1,0:T(8,128)(2,1)}, u32[]{:S(2)}) copy-start(bf16[128,640]{1,0:T(8,128)(2,1)} %param.9) | copy-start | bytes 491524
  43.9 48.3 %all-to-all-start.2 = ((bf16[32,40,640]{2,1,0:T(8,128)(2,1)}), bf16[32,40,640]{2,1,0:T(8,128)(2,1)}, u32[]{:S(2)}, u32[]{:S(2)}) async-start(bf16[32,40,640]{2,1,0:T(8,128)(2,1)} %bitcast.6), calls=%async_computation.2 | async-start | bytes 3276800 | tf_op jit(solution)/shard_map/all_to_all | solution.py:47
  92.2 44.6 %all-to-all-start.1 = ((bf16[32,40,640]{2,1,0:T(8,128)(2,1)}), bf16[32,40,640]{2,1,0:T(8,128)(2,1)S(1)}, u32[]{:S(2)}, u32[]{:S(2)}) async-start(bf16[32,40,640]{2,1,0:T(8,128)(2,1)} %bitcast.88), calls=%async_computation.1 | async-start | bytes 3276800 | tf_op jit(solution)/shard_map/all_to_all | solution.py:54
  96.4 676.1 %all-reduce.3.cloned.1.call-start = ((), (), s32[]{:S(2)}) async-start(), calls=%async_computation.6 | async-start | bytes 15728640 | tf_op jit(solution)/shard_map/psum | solution.py:78
  96.5 5.3 copy-start.10
  136.7 1.3 copy-start.9
  772.5 5.3 copy-start.1
  772.5 5.3 copy-start.2
  772.5 5.3 copy-start.3
  781.3 4.6 copy-start.4
  781.3 4.6 copy-start.6
  795.5 123.1 %all-to-all-start.4 = ((bf16[1,3,640,1024]{3,1,0,2:T(4,128)(2,1)}), bf16[1,3,640,1024]{3,1,0,2:T(4,128)(2,1)}, u32[]{:S(2)}, u32[]{:S(2)}) async-start(bf16[1,3,640,1024]{3,1,0,2:T(4,128)(2,1)} %copy.24), calls=%async_computation.4 | async-start | bytes 10485760 | tf_op jit(solution)/shard_map/all_to_all | solution.py:107
  801.8 4.2 copy-start.5
  801.8 4.2 copy-start.11
  809.5 113.9 %copy-start.8 = (s32[32]{0:T(128)S(1)}, s32[32]{0:T(128)}, u32[]{:S(2)}) copy-start(s32[32]{0:T(128)} %param.12) | copy-start | bytes 388
  918.6 45.2 %all-to-all-start.3 = ((bf16[32,40,640]{2,1,0:T(8,128)(2,1)}), bf16[32,40,640]{2,1,0:T(8,128)(2,1)S(1)}, u32[]{:S(2)}, u32[]{:S(2)}) async-start(bf16[32,40,640]{2,1,0:T(8,128)(2,1)} %bitcast.89), calls=%async_computation.3 | async-start | bytes 3276800 | tf_op jit(solution)/shard_map/all_to_all | solution.py:91
  963.8 111.1 %all-to-all-start.5 = ((bf16[32,3,20,1024]{3,2,1,0:T(8,128)(2,1)}), bf16[32,3,20,1024]{3,2,1,0:T(8,128)(2,1)}, u32[]{:S(2)}, u32[]{:S(2)}) async-start(bf16[32,3,20,1024]{3,2,1,0:T(8,128)(2,1)} %copy.27), calls=%async_computation.5 | async-start | bytes 9437184 | tf_op jit(solution)/shard_map/all_to_all | solution.py:110
Sparse Core Ops, SparseCore 0:
  141.9 630.5 all-reduce.2
where the time goes:
time: 1110 us; the launch traced here: 1100 us
  waiting for transfers between devices  926 us (83%)
  local copies, waits for them, and re-layouts  63 us (6%)
  matrix products  42.9 us (4%)
  starting transfers between devices  39 us (4%)
  between operations  14.6 us (1%)
  other arithmetic  12.7 us (1%)
    psum x1, waiting for transfers between devices, per_device(): lax.psum(up_part.astype(jnp.bfloat16), 'grp').astype(jnp.float32)  629 us
    all_to_all x1, waiting for transfers between devices, per_device(): lax.all_to_all(stacked, 'ep', split_axis=2, concat_axis=0, tiled=True)  109 us
    all_to_all x1, waiting for transfers between devices, per_device(): lax.all_to_all(mixed, 'ep', split_axis=0, concat_axis=2, tiled=True)  98.6 us
    all_to_all x1, waiting for transfers between devices, per_device(): lax.all_to_all(send_tokens.reshape(num_slots, capacity, width_part), 'ep'...  31.3 us
    all_to_all x1, waiting for transfers between devices, per_device(): lax.all_to_all(send_grads.reshape(num_slots, capacity, width_part), 'ep',...  29.8 us
    all_to_all x1, waiting for transfers between devices, per_device(): lax.all_to_all(row_grad.reshape(num_slots, capacity, width_part), 'ep', s...  28 us
  transfers between devices with their start and end apart: 7, of which 6 were waited for; matrix products, arithmetic and copies ran while one was open for 5% of the time, Pallas kernels for 0%

commit v1 on v0

v1 whole, which is shorter than its diff:
```python
import jax
import jax.numpy as jnp
from jax import lax
from jax.sharding import Mesh, PartitionSpec as P

EP = ("x", "zl", "c")
GRP = ("y", "zh")
BF = jnp.bfloat16
F32 = jnp.float32
CAP = 40


def dot(a, b, dims=((1,), (0,))):
    return lax.dot_general(a, b, (dims, ((), ())), preferred_element_type=F32)


def activate(gate, up_sum, grad_hidden):
    sigma = jax.nn.sigmoid(gate)
    swish = gate * sigma
    hidden = (swish * up_sum).astype(BF)
    grad_up = (grad_hidden * swish).astype(BF)
    grad_gate = (grad_hidden * up_sum * sigma * (1.0 + gate * (1.0 - sigma))).astype(BF)
    return (hidden, grad_gate, grad_up)


def routing(ids, probs, slot_expert):
    count = ids.shape[0]
    slots = slot_expert.shape[0]
    named = ids[:, :, None] == slot_expert[None, None, :]
    sent = jnp.any(named, axis=1)
    weight = jnp.sum(jnp.where(named, probs.astype(F32)[:, :, None], 0.0), axis=1)
    row = lax.broadcasted_iota(jnp.int32, (count, count), 0)
    col = lax.broadcasted_iota(jnp.int32, (count, count), 1)
    pos = dot((row > col).astype(BF), sent.astype(BF)).astype(jnp.int32)
    pos = jnp.where(sent, pos, -1)
    place = lax.broadcasted_iota(jnp.int32, (slots, CAP, count), 1)
    hit = pos.T[:, None, :] == place
    pick = hit.astype(BF).reshape(slots * CAP, count)
    scaled = jnp.where(hit, weight.T[:, None, :], 0.0).astype(BF).reshape(slots * CAP, count)
    slot = jnp.arange(slots)
    same = (slot_expert[:, None] == slot_expert[None, :]) & (slot[:, None] > slot[None, :])
    first = jnp.logical_not(jnp.any(same, axis=1))
    back = (hit & first[:, None, None]).astype(BF).reshape(slots * CAP, count)
    return pick, scaled, back


def swap_half(part):
    half = part.shape[0] // 2
    me = lax.axis_index("zh")
    keep = lax.dynamic_slice_in_dim(part, me * half, half, 0)
    give = lax.dynamic_slice_in_dim(part, (1 - me) * half, half, 0)
    got = lax.ppermute(give, "zh", [(0, 1), (1, 0)])
    return keep.astype(F32) + got.astype(F32)


def join_half(own):
    me = lax.axis_index("zh")
    other = lax.ppermute(own, "zh", [(0, 1), (1, 0)])
    lo = jnp.where(me == 0, own, other)
    hi = jnp.where(me == 0, other, own)
    return jnp.concatenate([lo, hi], axis=0)


def per_device(tokens, out_grad, expert_ids, route_probs, slot_expert, w_gate, w_up, w_down):
    width = tokens.shape[1]
    slots = slot_expert.shape[0]
    rows = slots * CAP
    pick, scaled, back = routing(expert_ids, route_probs, slot_expert)
    send_x = dot(pick, tokens).astype(BF).reshape(slots, CAP, width)
    send_g = dot(scaled, out_grad).astype(BF).reshape(slots, CAP, width)
    xs = lax.all_to_all(send_x, EP, 0, 0, tiled=True).reshape(rows, width)
    gs = lax.all_to_all(send_g, EP, 0, 0, tiled=True).reshape(rows, width)
    wg, wu, wd = w_gate[0], w_up[0], w_down[0]

    def total(part):
        return swap_half(lax.psum_scatter(part.astype(BF), "y", scatter_dimension=0, tiled=True))

    gate = total(dot(xs, wg))
    up = total(dot(xs, wu))
    dh = total(dot(gs, wd))
    hidden, d_gate, d_up = activate(gate, up, dh)

    def whole(own):
        return lax.all_gather(join_half(own), "y", axis=0, tiled=True)

    d_gate, d_up, hidden = whole(d_gate), whole(d_up), whole(hidden)
    rg = (dot(d_gate, wg, ((1,), (1,))) + dot(d_up, wu, ((1,), (1,)))).astype(BF)
    ret = lax.all_to_all(rg.reshape(slots, CAP, width), EP, 0, 0, tiled=True).reshape(rows, width)
    pg = dot(xs, d_gate, ((0,), (0,))).astype(BF)
    pu = dot(xs, d_up, ((0,), (0,))).astype(BF)
    pd = dot(gs, hidden, ((0,), (0,))).astype(BF)
    in_grad = dot(back, ret, ((0,), (0,))).astype(BF)
    return in_grad, pg[None], pu[None], pd[None]


def solution(mesh):
    fine = Mesh(mesh.devices.reshape(4, 2, 4, 4, 2), ("y", "zh", "x", "zl", "c"))
    return jax.shard_map(
        per_device,
        mesh=fine,
        in_specs=(
            P(EP, GRP),
            P(EP, GRP),
            P(EP, None),
            P(EP, None),
            P(),
            P(EP, GRP, None),
            P(EP, GRP, None),
            P(EP, GRP, None),
        ),
        out_specs=(P(EP, GRP), P(EP, GRP, None), P(EP, GRP, None), P(EP, GRP, None)),
        check_vma=False,
    )
```

time: 1110 us -> 367 us (0.33); the launches traced: 1100 us -> 366 us
  waiting for transfers between devices: 926 us -> 159 us
  blocking collectives: 0 us -> 94.9 us
  local copies, waits for them, and re-layouts: 63 us -> 7.84 us
    psum x1 -> x0, waiting for transfers between devices: 629 us -> none  [per_device(): lax.psum(up_part.astype(jnp.bfloat16), 'grp').astype(jnp.float32)]
    all_to_all x6 -> x1, waiting for transfers between devices: 297 us -> 10.2 us  [per_device(): lax.all_to_all(rg.reshape(slots, CAP, width), EP, 0, 0, tiled=True)]
    all_to_all x0 -> x2, blocking collectives: none -> 94.9 us  [the longest x1 50.6 us: per_device(): xs = lax.all_to_all(send_x, EP, 0, 0, tiled=True).reshape(rows, width)]
    all_gather x0 -> x3, waiting for transfers between devices: none -> 69 us  [whole(): return lax.all_gather(join_half(own), 'y', axis=0, tiled=True)]
    reduce_scatter x0 -> x3, waiting for transfers between devices: none -> 44.8 us  [total(): lax.psum_scatter(part.astype(BF), 'y', scatter_dimension=0, tiled=True)]
    ppermute x0 -> x6, waiting for transfers between devices: none -> 34.8 us  [the longest x3 26.2 us: join_half(): other = lax.ppermute(own, 'zh', [(0, 1), (1, 0)])]
    ppermute x0 -> x6, starting transfers between devices: none -> 31.2 us  [the longest x3 16.1 us: join_half(): other = lax.ppermute(own, 'zh', [(0, 1), (1, 0)])]
    all_to_all x6 -> x1, starting transfers between devices: 39 us -> 8.1 us  [per_device(): lax.all_to_all(rg.reshape(slots, CAP, width), EP, 0, 0, tiled=True)]
  transfers between devices with their start and end apart: 7 -> 13, of which waited for: 6 -> 10; matrix products, arithmetic and copies ran while one was open for 5% -> 11% of each run, Pallas kernels for 0% -> 0%
where the time goes in v1:
time: 367 us; the launch traced here: 366 us
  waiting for transfers between devices  159 us (43%)
  blocking collectives  94.9 us (26%)
  matrix products  41.5 us (11%)
  starting transfers between devices  39.5 us (11%)
  between operations  14.3 us (4%)
  other arithmetic  9.28 us (3%)
  local copies, waits for them, and re-layouts  7.84 us (2%)
    all_gather x3, waiting for transfers between devices, whole(): return lax.all_gather(join_half(own), 'y', axis=0, tiled=True)  69 us
    all_to_all x1, blocking collectives, per_device(): xs = lax.all_to_all(send_x, EP, 0, 0, tiled=True).reshape(rows, width)  50.6 us
    reduce_scatter x3, waiting for transfers between devices, total(): lax.psum_scatter(part.astype(BF), 'y', scatter_dimension=0, tiled=True)  44.8 us
    all_to_all x1, blocking collectives, per_device(): gs = lax.all_to_all(send_g, EP, 0, 0, tiled=True).reshape(rows, width)  44.3 us
    dot_general x12, matrix products, dot(): return lax.dot_general(a, b, (dims, ((), ())), preferred_element_type=F32)  41.5 us
    ppermute x3, waiting for transfers between devices, join_half(): other = lax.ppermute(own, 'zh', [(0, 1), (1, 0)])  26.2 us
    ppermute x3, starting transfers between devices, join_half(): other = lax.ppermute(own, 'zh', [(0, 1), (1, 0)])  16.1 us
    ppermute x3, starting transfers between devices, swap_half(): got = lax.ppermute(give, 'zh', [(0, 1), (1, 0)])  15.1 us
  transfers between devices with their start and end apart: 13, of which 10 were waited for; matrix products, arithmetic and copies ran while one was open for 11% of the time, Pallas kernels for 0%

profile of v1, /device:TPU:1, one launch (start us, length us, event | category | flops | bytes accessed | tf_op | source)
XLA Modules:
  0.0 366.3 jit_solution(4789089606818968500)
XLA Ops:
  10.1 50.6 %all_to_all.15 = bf16[32,40,640]{2,1,0:T(8,128)(2,1)S(1)} all-to-all(bf16[32,40,640]{2,1,0:T(8,128)(2,1)S(1)} %bitcast.56), channel_id=1, replica_groups=mesh['y'=4,'zh'=2,'x'=4,'zl'=4,'c'=2] {'x','zl','c'}, dimensions={0} | all-to-all | bytes 3276800 | tf_op jit(solution)/shard_map/all_to_all | solution.py:71
  64.5 3.8 %convolution_convert_fusion.1 = bf16[1280,1024]{1,0:T(8,128)(2,1)} fusion(bf16[1280,640]{1,0:T(8,128)(2,1)S(1)} %bitcast.59, bf16[1,640,1024]{2,1,0:T(8,128)(2,1)S(1)} %copy-done), kind=kOutput, calls=%fused_computation.1 | convolution fusion | flops 1679032320 | bytes 5570560 | tf_op jit(solution)/shard_map/dot_general | solution.py:14
  69.9 44.3 %all_to_all.16 = bf16[32,40,640]{2,1,0:T(8,128)(2,1)S(1)} all-to-all(bf16[32,40,640]{2,1,0:T(8,128)(2,1)S(1)} %bitcast.57), channel_id=1, replica_groups=mesh['y'=4,'zh'=2,'x'=4,'zl'=4,'c'=2] {'x','zl','c'}, dimensions={0} | all-to-all | bytes 3276800 | tf_op jit(solution)/shard_map/all_to_all | solution.py:72
  121.0 4.2 %collective-permute-start.2 = (bf16[160,1024]{1,0:T(8,128)(2,1)}, bf16[160,1024]{1,0:T(8,128)(2,1)S(1)}, u32[]{:S(2)}, u32[]{:S(2)}) collective-permute-start(bf16[160,1024]{1,0:T(8,128)(2,1)} %constant_dynamic-slice_fusion), channel_id=1, source_target_pairs={{0,32},{32,0},{1,33},{33,1},{2,34},{34,2},{3,35},{35,3},{4,36},{36... | collective-permute-start | bytes 983048 | tf_op jit(solution)/shard_map/ppermute | solution.py:52
  125.2 13.1 %reduce-scatter.6.cloned.1.call-done = bf16[320,1024]{1,0:T(8,128)(2,1)} async-done(((bf16[1280,1024]{1,0:T(8,128)(2,1)}), bf16[320,1024]{1,0:T(8,128)(2,1)}) %reduce-scatter.6.cloned.1.call-update) | async-done | bytes 655376 | tf_op jit(solution)/shard_map/reduce_scatter | solution.py:76
  140.0 5.4 %collective-permute-start.1 = (bf16[160,1024]{1,0:T(8,128)(2,1)}, bf16[160,1024]{1,0:T(8,128)(2,1)}, u32[]{:S(2)}, u32[]{:S(2)}) collective-permute-start(bf16[160,1024]{1,0:T(8,128)(2,1)} %constant_dynamic-slice_fusion.1), channel_id=1, source_target_pairs={{0,32},{32,0},{1,33},{33,1},{2,34},{34,2},{3,35},{35,3},{4,36},{36... | collective-permute-start | bytes 983048 | tf_op jit(solution)/shard_map/ppermute | solution.py:52
  145.4 31.7 %reduce-scatter.4.cloned.1.call-done = bf16[320,1024]{1,0:T(8,128)(2,1)} async-done(((bf16[1280,1024]{1,0:T(8,128)(2,1)}), bf16[320,1024]{1,0:T(8,128)(2,1)}) %reduce-scatter.4.cloned.1.call-update) | async-done | bytes 655376 | tf_op jit(solution)/shard_map/reduce_scatter | solution.py:76
  178.9 5.4 %collective-permute-start = (bf16[160,1024]{1,0:T(8,128)(2,1)}, bf16[160,1024]{1,0:T(8,128)(2,1)}, u32[]{:S(2)}, u32[]{:S(2)}) collective-permute-start(bf16[160,1024]{1,0:T(8,128)(2,1)} %constant_dynamic-slice_fusion.2), channel_id=1, source_target_pairs={{0,32},{32,0},{1,33},{33,1},{2,34},{34,2},{3,35},{35,3},{4,36},{36... | collective-permute-start | bytes 983048 | tf_op jit(solution)/shard_map/ppermute | solution.py:52
  185.0 8.6 %collective-permute-done = bf16[160,1024]{1,0:T(8,128)(2,1)} collective-permute-done((bf16[160,1024]{1,0:T(8,128)(2,1)}, bf16[160,1024]{1,0:T(8,128)(2,1)}, u32[]{:S(2)}, u32[]{:S(2)}) %collective-permute-start) | collective-permute-done | bytes 327712 | tf_op jit(solution)/shard_map/ppermute | solution.py:52
  196.5 5.5 %collective-permute-start.4 = (bf16[160,1024]{1,0:T(8,128)(2,1)}, bf16[160,1024]{1,0:T(8,128)(2,1)}, u32[]{:S(2)}, u32[]{:S(2)}) collective-permute-start(bf16[160,1024]{1,0:T(8,128)(2,1)} %get-tuple-element.6), channel_id=1, source_target_pairs={{0,32},{32,0},{1,33},{33,1},{2,34},{34,2},{3,35},{35,3},{4,36},{36... | collective-permute-start | bytes 983048 | tf_op jit(solution)/shard_map/ppermute | solution.py:58
  201.9 4.8 %collective-permute-done.4 = bf16[160,1024]{1,0:T(8,128)(2,1)} collective-permute-done((bf16[160,1024]{1,0:T(8,128)(2,1)}, bf16[160,1024]{1,0:T(8,128)(2,1)}, u32[]{:S(2)}, u32[]{:S(2)}) %collective-permute-start.4) | collective-permute-done | bytes 327712 | tf_op jit(solution)/shard_map/ppermute | solution.py:58
  208.8 5.5 %collective-permute-start.3 = (bf16[160,1024]{1,0:T(8,128)(2,1)}, bf16[160,1024]{1,0:T(8,128)(2,1)S(1)}, u32[]{:S(2)}, u32[]{:S(2)}) collective-permute-start(bf16[160,1024]{1,0:T(8,128)(2,1)} %get-tuple-element.5), channel_id=1, source_target_pairs={{0,32},{32,0},{1,33},{33,1},{2,34},{34,2},{3,35},{35,3},{4,36},{36... | collective-permute-start | bytes 983048 | tf_op jit(solution)/shard_map/ppermute | solution.py:58
  214.3 9.8 %collective-permute-done.3 = bf16[160,1024]{1,0:T(8,128)(2,1)S(1)} collective-permute-done((bf16[160,1024]{1,0:T(8,128)(2,1)}, bf16[160,1024]{1,0:T(8,128)(2,1)S(1)}, u32[]{:S(2)}, u32[]{:S(2)}) %collective-permute-start.3) | collective-permute-done | bytes 327712 | tf_op jit(solution)/shard_map/ppermute | solution.py:58
  226.0 5.2 %collective-permute-start.5 = (bf16[160,1024]{1,0:T(8,128)(2,1)S(1)}, bf16[160,1024]{1,0:T(8,128)(2,1)S(1)}, u32[]{:S(2)}, u32[]{:S(2)}) collective-permute-start(bf16[160,1024]{1,0:T(8,128)(2,1)S(1)} %get-tuple-element.4), channel_id=1, source_target_pairs={{0,32},{32,0},{1,33},{33,1},{2,34},{34,2},{3,35},{35,3},{4,36},{36... | collective-permute-start | bytes 983048 | tf_op jit(solution)/shard_map/ppermute | solution.py:58
  231.1 11.7 %collective-permute-done.5 = bf16[160,1024]{1,0:T(8,128)(2,1)S(1)} collective-permute-done((bf16[160,1024]{1,0:T(8,128)(2,1)S(1)}, bf16[160,1024]{1,0:T(8,128)(2,1)S(1)}, u32[]{:S(2)}, u32[]{:S(2)}) %collective-permute-start.5) | collective-permute-done | bytes 327712 | tf_op jit(solution)/shard_map/ppermute | solution.py:58
  243.8 17.8 %all-gather.6.cloned.1.call-done = bf16[1280,1024]{1,0:T(8,128)(2,1)} async-done(((bf16[320,1024]{1,0:T(8,128)(2,1)}), bf16[1280,1024]{1,0:T(8,128)(2,1)}) %all-gather.6.cloned.1.call-update) | async-done | bytes 2621456 | tf_op jit(solution)/shard_map/all_gather | solution.py:84
  261.6 5.6 %fusion.6 = f32[1280,640]{1,0:T(8,128)} fusion(bf16[1280,1024]{1,0:T(8,128)(2,1)} %all-gather.6.cloned.1.call-done, bf16[1,640,1024]{2,1,0:T(8,128)(2,1)S(1)} %copy-done), kind=kOutput, calls=%fused_computation.15 | convolution fusion | flops 1677721600 | bytes 7208960 | tf_op jit(solution)/shard_map/dot_general | solution.py:14
  267.2 34.5 %all-gather.4.cloned.1.call-done = bf16[1280,1024]{1,0:T(8,128)(2,1)} async-done(((bf16[320,1024]{1,0:T(8,128)(2,1)}), bf16[1280,1024]{1,0:T(8,128)(2,1)}) %all-gather.4.cloned.1.call-update) | async-done | bytes 2621456 | tf_op jit(solution)/shard_map/all_gather | solution.py:84
  301.7 6.5 %fusion = bf16[1280,640]{1,0:T(8,128)(2,1)} fusion(f32[1280,640]{1,0:T(8,128)} %fusion.6, bf16[1280,1024]{1,0:T(8,128)(2,1)} %all-gather.4.cloned.1.call-done, bf16[1,640,1024]{2,1,0:T(8,128)(2,1)} %param.13), kind=kOutput, calls=%fused_computation.5 | convolution fusion | flops 1679360000 | bytes 8847360 | tf_op jit(solution)/shard_map/dot_general | solution.py:14
  308.2 8.1 %all-to-all-start.2 = ((bf16[32,40,640]{2,1,0:T(8,128)(2,1)}), bf16[32,40,640]{2,1,0:T(8,128)(2,1)}, u32[]{:S(2)}, u32[]{:S(2)}) async-start(bf16[32,40,640]{2,1,0:T(8,128)(2,1)} %bitcast.64), calls=%async_computation.5 | async-start | bytes 3276800 | tf_op jit(solution)/shard_map/all_to_all | solution.py:88
  316.5 5.0 %fusion.2 = bf16[1,640,1024]{2,1,0:T(8,128)(2,1)} fusion(bf16[1280,640]{1,0:T(8,128)(2,1)S(1)} %bitcast.60, bf16[1280,1024]{1,0:T(8,128)(2,1)} %all-gather.6.cloned.1.call-done), kind=kOutput, calls=%fused_computation.11 | convolution fusion | flops 1678376960 | bytes 5570560 | tf_op jit(solution)/shard_map/dot_general | solution.py:14
  324.5 16.7 %all-gather.8.cloned.1.call-done = bf16[1280,1024]{1,0:T(8,128)(2,1)} async-done(((bf16[320,1024]{1,0:T(8,128)(2,1)}), bf16[1280,1024]{1,0:T(8,128)(2,1)}) %all-gather.8.cloned.1.call-update) | async-done | bytes 2621456 | tf_op jit(solution)/shard_map/all_gather | solution.py:84
  341.3 5.2 %fusion.3 = bf16[1,640,1024]{2,1,0:T(8,128)(2,1)} fusion(bf16[1280,640]{1,0:T(8,128)(2,1)} %bitcast.63, bf16[1280,1024]{1,0:T(8,128)(2,1)} %all-gather.8.cloned.1.call-done), kind=kOutput, calls=%fused_computation.12 | convolution fusion | flops 1678376960 | bytes 5570560 | tf_op jit(solution)/shard_map/dot_general | solution.py:14
  346.5 10.2 %all-to-all-done.2 = bf16[32,40,640]{2,1,0:T(8,128)(2,1)} async-done(((bf16[32,40,640]{2,1,0:T(8,128)(2,1)}), bf16[32,40,640]{2,1,0:T(8,128)(2,1)}, u32[]{:S(2)}, u32[]{:S(2)}) %all-to-all-start.2) | async-done | bytes 1638432 | tf_op jit(solution)/shard_map/all_to_all | solution.py:88
  (61 shorter events, 32.9 us)
Async XLA Ops:
  7.2 57.4 %copy-start = (bf16[1,640,1024]{2,1,0:T(8,128)(2,1)S(1)}, bf16[1,640,1024]{2,1,0:T(8,128)(2,1)}, u32[]{:S(2)}) copy-start(bf16[1,640,1024]{2,1,0:T(8,128)(2,1)} %param.14) | copy-start | bytes 3932164
  7.2 112.1 %reduce-scatter.8.cloned.1.call-start = ((), (), s32[]{:S(2)}) async-start(), calls=%async_computation.8 | async-start | bytes 3276800 | tf_op jit(solution)/shard_map/reduce_scatter | solution.py:76
  10.1 50.6 %copy-start.9 = (bf16[1,640,1024]{2,1,0:T(8,128)(2,1)S(1)}, bf16[1,640,1024]{2,1,0:T(8,128)(2,1)}, u32[]{:S(2)}) copy-start(bf16[1,640,1024]{2,1,0:T(8,128)(2,1)} %param.13) | copy-start | bytes 3932164
  64.5 73.8 %reduce-scatter.6.cloned.1.call-start = ((), (), s32[]{:S(2)}) async-start(), calls=%async_computation.7 | async-start | bytes 3276800 | tf_op jit(solution)/shard_map/reduce_scatter | solution.py:76
  68.3 0.7 copy-start.5
  68.3 0.7 copy-start.4
  68.3 0.7 copy-start.6
  68.3 1.0 copy-start.3
  68.3 108.8 %reduce-scatter.4.cloned.1.call-start = ((), (), s32[]{:S(2)}) async-start(), calls=%async_computation.6 | async-start | bytes 3276800 | tf_op jit(solution)/shard_map/reduce_scatter | solution.py:76
  69.9 45.5 %copy-start.8 = (bf16[1,640,1024]{2,1,0:T(8,128)(2,1)S(1)}, bf16[1,640,1024]{2,1,0:T(8,128)(2,1)}, u32[]{:S(2)}) copy-start(bf16[1,640,1024]{2,1,0:T(8,128)(2,1)} %param.15) | copy-start | bytes 3932164
  114.2 1.2 copy-start.1
  119.2 142.4 %all-gather.6.cloned.1.call-start = ((), (), s32[]{:S(2)}) async-start(), calls=%async_computation.10 | async-start | bytes 3276800 | tf_op jit(solution)/shard_map/all_gather | solution.py:84
  121.0 63.3 %collective-permute-start.2 = (bf16[160,1024]{1,0:T(8,128)(2,1)}, bf16[160,1024]{1,0:T(8,128)(2,1)S(1)}, u32[]{:S(2)}, u32[]{:S(2)}) collective-permute-start(bf16[160,1024]{1,0:T(8,128)(2,1)} %constant_dynamic-slice_fusion), channel_id=1, source_target_pairs={{0,32},{32,0},{1,33},{33,1},{2,34},{34,2},{3,35},{35,3},{4,36},{36... | collective-permute-start | bytes 983048 | tf_op jit(solution)/shard_map/ppermute | solution.py:52
  140.0 44.3 %collective-permute-start.1 = (bf16[160,1024]{1,0:T(8,128)(2,1)}, bf16[160,1024]{1,0:T(8,128)(2,1)}, u32[]{:S(2)}, u32[]{:S(2)}) collective-permute-start(bf16[160,1024]{1,0:T(8,128)(2,1)} %constant_dynamic-slice_fusion.1), channel_id=1, source_target_pairs={{0,32},{32,0},{1,33},{33,1},{2,34},{34,2},{3,35},{35,3},{4,36},{36... | collective-permute-start | bytes 983048 | tf_op jit(solution)/shard_map/ppermute | solution.py:52
  178.9 14.8 %collective-permute-start = (bf16[160,1024]{1,0:T(8,128)(2,1)}, bf16[160,1024]{1,0:T(8,128)(2,1)}, u32[]{:S(2)}, u32[]{:S(2)}) collective-permute-start(bf16[160,1024]{1,0:T(8,128)(2,1)} %constant_dynamic-slice_fusion.2), channel_id=1, source_target_pairs={{0,32},{32,0},{1,33},{33,1},{2,34},{34,2},{3,35},{35,3},{4,36},{36... | collective-permute-start | bytes 983048 | tf_op jit(solution)/shard_map/ppermute | solution.py:52
  184.3 0.7 copy-start.2
  196.5 10.2 %collective-permute-start.4 = (bf16[160,1024]{1,0:T(8,128)(2,1)}, bf16[160,1024]{1,0:T(8,128)(2,1)}, u32[]{:S(2)}, u32[]{:S(2)}) collective-permute-start(bf16[160,1024]{1,0:T(8,128)(2,1)} %get-tuple-element.6), channel_id=1, source_target_pairs={{0,32},{32,0},{1,33},{33,1},{2,34},{34,2},{3,35},{35,3},{4,36},{36... | collective-permute-start | bytes 983048 | tf_op jit(solution)/shard_map/ppermute | solution.py:58
  208.7 93.0 %all-gather.4.cloned.1.call-start = ((), (), s32[]{:S(2)}) async-start(), calls=%async_computation.9 | async-start | bytes 3276800 | tf_op jit(solution)/shard_map/all_gather | solution.py:84
  208.8 15.2 %collective-permute-start.3 = (bf16[160,1024]{1,0:T(8,128)(2,1)}, bf16[160,1024]{1,0:T(8,128)(2,1)S(1)}, u32[]{:S(2)}, u32[]{:S(2)}) collective-permute-start(bf16[160,1024]{1,0:T(8,128)(2,1)} %get-tuple-element.5), channel_id=1, source_target_pairs={{0,32},{32,0},{1,33},{33,1},{2,34},{34,2},{3,35},{35,3},{4,36},{36... | collective-permute-start | bytes 983048 | tf_op jit(solution)/shard_map/ppermute | solution.py:58
  225.9 115.3 %all-gather.8.cloned.1.call-start = ((), (), s32[]{:S(2)}) async-start(), calls=%async_computation.11 | async-start | bytes 3276800 | tf_op jit(solution)/shard_map/all_gather | solution.py:84
  226.0 16.8 %collective-permute-start.5 = (bf16[160,1024]{1,0:T(8,128)(2,1)S(1)}, bf16[160,1024]{1,0:T(8,128)(2,1)S(1)}, u32[]{:S(2)}, u32[]{:S(2)}) collective-permute-start(bf16[160,1024]{1,0:T(8,128)(2,1)S(1)} %get-tuple-element.4), channel_id=1, source_target_pairs={{0,32},{32,0},{1,33},{33,1},{2,34},{34,2},{3,35},{35,3},{4,36},{36... | collective-permute-start | bytes 983048 | tf_op jit(solution)/shard_map/ppermute | solution.py:58
  308.2 48.4 %all-to-all-start.2 = ((bf16[32,40,640]{2,1,0:T(8,128)(2,1)}), bf16[32,40,640]{2,1,0:T(8,128)(2,1)}, u32[]{:S(2)}, u32[]{:S(2)}) async-start(bf16[32,40,640]{2,1,0:T(8,128)(2,1)} %bitcast.64), calls=%async_computation.5 | async-start | bytes 3276800 | tf_op jit(solution)/shard_map/all_to_all | solution.py:88
  316.5 5.0 %copy-start.7 = (bf16[1280,1024]{1,0:T(8,128)(2,1)S(1)}, bf16[1280,1024]{1,0:T(8,128)(2,1)}, u32[]{:S(2)}) copy-start(bf16[1280,1024]{1,0:T(8,128)(2,1)} %all-gather.4.cloned.1.call-done) | copy-start | bytes 7864324
Sparse Core Ops, SparseCore 0:
  64.6 34.7 reduce-scatter.7
  101.9 36.2 reduce-scatter.5
  140.8 36.2 reduce-scatter.3
  208.9 52.6 all-gather.5
  263.8 37.8 all-gather.3
  303.4 37.8 all-gather.7
